TPU v7x, 32 devices: a whole 2x2x4 slice. The times are simulated.
32 devices in a mesh: level: 2 (over y), lon: 8 (over z, x), lat: 2 (over core).
Axes of the slice: x: 2, y: 2, z: 4, core: 2. Of those that a mesh axis runs over, the one named last changes fastest.
Arguments:
- wind_snaps: float32 [4, 32, 32, 256], P('level', None, 'lon', 'lat'), parts along dimension 0, may hold values from -48 to 48
- old_basis: float32 [4, 64, 32, 256], P('level', None, 'lon', 'lat'), parts along dimension 0, may hold values from -17 to 17
- old_values: float32 [4, 64], P('level'), parts along dimension 0, may hold values from 1 to 4
Outputs:
- new_basis: float32 [4, 64, 32, 256], P('level', None, 'lon', 'lat'), parts along dimension 0
- new_values: float32 [4, 64], P('level'), parts along dimension 0
There are 2 independent parts, one for each index of `level`. A program takes and returns all parts, laid end to end along the dimension named above; each array names one. Nothing has to cross between parts.
All inputs are finite; a program needn't handle non-finite values.
Results may differ from a plain program's by a relative error of at most 0.00012.
Values sent between devices are 32-bit elements; how exact they have to be, the bound alone decides.
A program may use at most 64 MiB of HBM per device.

v0:
```python
import jax
import jax.numpy as jnp
from jax import lax
from jax.sharding import PartitionSpec as P

ITERS = 2
FULL_PRECISION = lax.Precision.HIGHEST


def extended(value, sides, width, wrap):
    for axis, dim in sides:
        count, length = (lax.axis_size(axis), value.shape[dim])
        up = [(i, (i + 1) % count) for i in range(count if wrap else count - 1)]
        down = [(j, i) for i, j in up]
        last = lax.slice_in_dim(value, length - width, length, axis=dim)
        first = lax.slice_in_dim(value, 0, width, axis=dim)
        before = lax.ppermute(last, axis, up)
        after = lax.ppermute(first, axis, down)
        value = jnp.concatenate([before, value, after], axis=dim)
    return value


def cholesky_pair(matrix):
    order = matrix.shape[0]
    positions = jnp.arange(order, dtype=jnp.int32)

    def row_step(row, carry):
        lower, inverse = carry
        column = lax.dynamic_slice_in_dim(matrix, row, 1, 1)[:, 0]
        partial_row = jnp.dot(inverse, column, precision=FULL_PRECISION)
        diag_entry = lax.dynamic_slice_in_dim(column, row, 1, 0)[0]
        pivot = jnp.sqrt(diag_entry - jnp.sum(partial_row * partial_row))
        unit = (positions == row).astype(matrix.dtype)
        lower_row = partial_row + pivot * unit
        inverse_row = (unit - jnp.dot(partial_row, inverse, precision=FULL_PRECISION)) / pivot
        lower = lax.dynamic_update_slice_in_dim(lower, lower_row[None], row, 0)
        inverse = lax.dynamic_update_slice_in_dim(inverse, inverse_row[None], row, 0)
        return (lower, inverse)

    return lax.fori_loop(0, order, row_step, (jnp.zeros_like(matrix), jnp.zeros_like(matrix)))


def project_one(gram_uu, gram_ua):
    factor_low, low_inverse = cholesky_pair(gram_uu)
    projected = jnp.dot(low_inverse, gram_ua, precision=FULL_PRECISION)
    lifted = jnp.dot(low_inverse.T, projected, precision=FULL_PRECISION)
    return (low_inverse, projected, lifted)


def upper_pair(gram):
    lower, inverse = cholesky_pair(gram)
    return (lower.T, inverse.T)


def rotate_one(low_inverse, projected, factor_up, up_inverse, values):
    rank_count = values.shape[0]
    snap_count = factor_up.shape[0]
    top_rows = jnp.concatenate([jnp.diag(values), projected], axis=1)
    bottom_rows = jnp.concatenate(
        [jnp.zeros((snap_count, rank_count), jnp.float32), factor_up], axis=1
    )
    joint_matrix = jnp.concatenate([top_rows, bottom_rows], axis=0)
    square = jnp.dot(joint_matrix, joint_matrix.T, precision=FULL_PRECISION)
    subspace = jnp.eye(rank_count + snap_count, rank_count, dtype=jnp.float32)
    for sweep in range(ITERS):
        applied = jnp.dot(square, subspace, precision=FULL_PRECISION)
        inner = jnp.dot(applied.T, applied, precision=FULL_PRECISION)
        chol_low, chol_inverse = cholesky_pair(inner)
        subspace = jnp.dot(applied, chol_inverse.T, precision=FULL_PRECISION)
    energy = jnp.sum(subspace * jnp.dot(square, subspace, precision=FULL_PRECISION), axis=0)
    new_values = jnp.sqrt(energy)
    mix_old = jnp.dot(low_inverse.T, subspace[:rank_count], precision=FULL_PRECISION).T
    mix_new = jnp.dot(up_inverse, subspace[rank_count:], precision=FULL_PRECISION).T
    return (mix_old, mix_new, new_values)


def residual_rows(fields, basis_rows, lifted):
    return fields - jnp.einsum("fks,fkc->fsc", lifted, basis_rows, precision=FULL_PRECISION)


def per_device(wind_snaps, old_basis, old_values):
    snap_count = wind_snaps.shape[1]
    rank_count = old_basis.shape[1]
    lon_cells = wind_snaps.shape[2]
    lat_cells = wind_snaps.shape[3]
    rows_all = lat_cells * lax.axis_size("lat")
    cell_count = lon_cells * lax.axis_size("lon") * rows_all
    row_place = (lax.axis_index("lat") * lat_cells + jnp.arange(lat_cells, dtype=jnp.int32)).astype(
        jnp.float32
    )
    cosines = jnp.cos(((row_place + 0.5) / rows_all - 0.5) * (jnp.pi / 2.0))
    lon_padded = extended(wind_snaps, (("lon", 2),), 1, True)
    lat_padded = extended(wind_snaps * cosines, (("lat", 3),), 1, False)
    lon_diff = lon_padded[:, :, 2:, :] - lon_padded[:, :, :-2, :]
    lat_diff = lat_padded[:, :, :, 2:] - lat_padded[:, :, :, :-2]
    twice_cos = 2.0 * cosines
    vorticity = (lon_diff[1] - lat_diff[0]) / twice_cos
    divergence = (lon_diff[0] + lat_diff[1]) / twice_cos
    fields = jnp.stack([vorticity, divergence]).reshape(2, snap_count, lon_cells * lat_cells)
    basis_rows = old_basis.reshape(2, rank_count, lon_cells * lat_cells)
    local_uu = jnp.einsum("fkc,fjc->fkj", basis_rows, basis_rows, precision=FULL_PRECISION)
    local_ua = jnp.einsum("fkc,fsc->fks", basis_rows, fields, precision=FULL_PRECISION)
    sum_uu, sum_ua = lax.psum((local_uu, local_ua), ("lon", "lat"))
    low_inverse, projected, lifted = jax.vmap(project_one)(sum_uu / cell_count, sum_ua / cell_count)
    residual = residual_rows(fields, basis_rows, lifted)
    local_rr = jnp.einsum("fsc,ftc->fst", residual, residual, precision=FULL_PRECISION)
    sum_rr = lax.psum(local_rr, ("lon", "lat"))
    factor_up, up_inverse = jax.vmap(upper_pair)(sum_rr / cell_count)
    mix_old, mix_new, new_values = jax.vmap(rotate_one)(
        low_inverse, projected, factor_up, up_inverse, old_values
    )
    new_basis = jnp.einsum("fkj,fjc->fkc", mix_old, basis_rows, precision=FULL_PRECISION)
    new_basis = new_basis + jnp.einsum("fks,fsc->fkc", mix_new, residual, precision=FULL_PRECISION)
    return (new_basis.reshape(2, rank_count, lon_cells, lat_cells), new_values)


def solution(mesh):
    placed = (P("level", None, "lon", "lat"), P("level", None, "lon", "lat"), P("level", None))
    return jax.shard_map(
        per_device,
        mesh=mesh,
        in_specs=placed,
        out_specs=(P("level", None, "lon", "lat"), P("level", None)),
        check_vma=False,
    )
```

profile of v0, /device:TPU:0, one launch (start us, length us, event | category | flops | bytes accessed | tf_op | source)
XLA Modules:
  0.0 1083.0 jit_solution(2098849238049554596)
XLA Ops:
  0.6 1.0 fusion.76
  1.7 6.0 collective-permute-start
  7.7 1.1 reshape.448
  10.0 4.3 collective-permute-done.1
  14.3 1.2 fusion.47
  15.7 1.3 collective-permute-start.2
  17.0 3.0 collective-permute-start.3
  20.1 0.9 collective-permute-done.3
  21.7 58.7 %all-reduce.1 = (f32[2,64,64]{2,1,0:T(8,128)S(1)}, f32[2,64,32]{1,2,0:T(8,128)S(1)}) all-reduce(f32[2,64,64]{2,1,0:T(8,128)S(1)} %fusion.78, f32[2,64,32]{1,2,0:T(8,128)S(1)} %convolution_bitcast_fusion), channel_id=1, replica_groups=mesh['level'=2,'lon'=8,'lat'=2] {'lon','lat'}, use_global_device_ids=true, to_apply=%region_0.0 | all-reduce | flops 12288 | bytes 98304 | tf_op jit(solution)/shard_map/psum | solution.py:103
  81.2 268.9 %while.71 = (s32[]{:T(128)}, f32[2,64,64]{2,0,1:T(2,128)S(1)}, f32[2,64,64]{0,2,1:T(8,128)S(1)}, s32[]{:T(128)}, s32[2]{0:T(128)S(1)}, /*index=5*/s32[1]{0:T(128)}, s32[3]{0:T(128)S(1)}, s32[]{:T(128)}, s32[]{:T(128)}) while((s32[]{:T(128)}, f32[2,64,64]{2,0,1:T(2,128)S(1)}, f32[2,64,64]{0,2,1:T(8,128)S(1)}, s32[]{:T(128)}, ...), condition=%wide.region_4.5_spmd.clone, body=%wide.region_1.4_spmd.clone.sunk | while | flops 197400 | bytes 75255 | solution.py:40
  351.3 57.6 %psum.23 = f32[2,32,32]{2,1,0:T(8,128)S(1)} all-reduce(f32[2,32,32]{2,1,0:T(8,128)S(1)} %fusion.80), channel_id=1, replica_groups=mesh['level'=2,'lon'=8,'lat'=2] {'lon','lat'}, use_global_device_ids=true, to_apply=%region_6.0 | all-reduce | flops 2048 | bytes 16384 | tf_op jit(solution)/shard_map/psum | solution.py:107
  409.3 131.4 %while.72 = (s32[]{:T(128)}, f32[2,32,32]{2,0,1:T(2,128)S(1)}, f32[2,32,32]{2,0,1:T(2,128)S(1)}, f32[2,32,32]{0,2,1:T(8,128)S(1)}, s32[]{:T(128)}, /*index=5*/s3...) while((s32[]{:T(128)}, f32[2,32,32]{2,0,1:T(2,128)S(1)}, ...), condition=%wide.region_10.11_spmd.clone, body=%wide.region_7.10_spmd.clone.sunk | while | flops 49752 | bytes 26751 | solution.py:40
  412.6 0.8 constant_dynamic-update-slice_fusion.5
  416.7 0.8 constant_dynamic-update-slice_fusion.5
  420.8 0.8 constant_dynamic-update-slice_fusion.5
  424.9 0.8 constant_dynamic-update-slice_fusion.5
  429.0 0.8 constant_dynamic-update-slice_fusion.5
  433.1 0.8 constant_dynamic-update-slice_fusion.5
  437.2 0.8 constant_dynamic-update-slice_fusion.5
  449.6 0.8 constant_dynamic-update-slice_fusion.5
  453.7 0.8 constant_dynamic-update-slice_fusion.5
  457.8 0.8 constant_dynamic-update-slice_fusion.5
  461.9 0.8 constant_dynamic-update-slice_fusion.5
  466.0 0.8 constant_dynamic-update-slice_fusion.5
  470.1 0.8 constant_dynamic-update-slice_fusion.5
  474.2 0.8 constant_dynamic-update-slice_fusion.5
  486.5 0.8 constant_dynamic-update-slice_fusion.5
  490.6 0.8 constant_dynamic-update-slice_fusion.5
  494.7 0.8 constant_dynamic-update-slice_fusion.5
  542.4 267.9 %while.73 = (s32[]{:T(128)}, f32[2,64,64]{2,0,1:T(2,128)S(1)}, f32[2,64,64]{0,2,1:T(8,128)S(1)}, s32[]{:T(128)}, s32[2]{0:T(128)S(1)}, /*index=5*/s32[1]{0:T(128)}, s32[3]{0:T(128)S(1)}, s32[]{:T(128)}, s32[]{:T(128)}) while((s32[]{:T(128)}, f32[2,64,64]{2,0,1:T(2,128)S(1)}, f32[2,64,64]{0,2,1:T(8,128)S(1)}, s32[]{:T(128)}, ...), condition=%wide.region_14.15_spmd.clone, body=%wide.region_11.14_spmd.clone.sunk | while | flops 197400 | bytes 75255 | solution.py:40
  811.8 267.9 %while.74 = (s32[]{:T(128)}, f32[2,64,64]{2,0,1:T(2,128)S(1)}, f32[2,64,64]{0,2,1:T(8,128)S(1)}, s32[]{:T(128)}, s32[2]{0:T(128)S(1)}, /*index=5*/s32[1]{0:T(128)}, s32[3]{0:T(128)S(1)}, s32[]{:T(128)}, s32[]{:T(128)}) while((s32[]{:T(128)}, f32[2,64,64]{2,0,1:T(2,128)S(1)}, f32[2,64,64]{0,2,1:T(8,128)S(1)}, s32[]{:T(128)}, ...), condition=%wide.region_18.19_spmd.clone, body=%wide.region_15.0_spmd.clone.sunk | while | flops 197400 | bytes 75255 | solution.py:40
  1082.3 0.8 reshape.449
  (2726 shorter events, 778.7 us)
Async XLA Ops:
  1.7 8.3 collective-permute-start
  7.7 6.6 collective-permute-start.1
  15.7 4.4 collective-permute-start.2
  17.0 4.0 collective-permute-start.3
  20.1 61.2 %copy-start = (s32[2]{0:T(128)S(1)}, s32[2]{0:T(128)}, u32[]{:S(2)}) copy-start(s32[2]{0:T(128)} %constant.357.clone.2) | copy-start | bytes 28
  20.1 61.2 %copy-start.1 = (s32[3]{0:T(128)S(1)}, s32[3]{0:T(128)}, u32[]{:S(2)}) copy-start(s32[3]{0:T(128)} %constant.358.clone.2) | copy-start | bytes 40
  81.2 328.1 %copy-start.2 = (s32[2]{0:T(128)S(1)}, s32[2]{0:T(128)}, u32[]{:S(2)}) copy-start(s32[2]{0:T(128)} %constant.365.clone.2) | copy-start | bytes 28
  81.2 328.1 %copy-start.3 = (s32[3]{0:T(128)S(1)}, s32[3]{0:T(128)}, u32[]{:S(2)}) copy-start(s32[3]{0:T(128)} %constant.366.clone.2) | copy-start | bytes 40
where the time goes:
time: 1090 us; the launch traced here: 1080 us
  other arithmetic  404 us (37%)
  local copies, waits for them, and re-layouts  308 us (28%)
  loops' own time  154 us (14%)
  blocking collectives  116 us (11%)
  matrix products  84 us (8%)
    while x448, local copies, waits for them, and re-layouts, row_step(): column = lax.dynamic_slice_in_dim(matrix, row, 1, 1)[:, 0]  286 us
    scatter x224, other arithmetic, row_step(): lax.dynamic_update_slice_in_dim(inverse, inverse_row[None], row, 0)  170 us
    another operation x224, other arithmetic  163 us
    another operation x4, loops' own time, cholesky_pair(): lax.fori_loop(0, order, row_step, (jnp.zeros_like(matrix), jnp.zeros_like...  154 us
    psum x1, blocking collectives, per_device(): sum_uu, sum_ua = lax.psum((local_uu, local_ua), ('lon', 'lat'))  58.7 us
    psum x1, blocking collectives, per_device(): sum_rr = lax.psum(local_rr, ('lon', 'lat'))  57.6 us
    dot_general x224, matrix products, row_step(): partial_row = jnp.dot(inverse, column, precision=FULL_PRECISION)  43.8 us
    dot_general x224, matrix products, row_step(): jnp.dot(partial_row, inverse, precision=FULL_PRECISION)  35.1 us
  transfers between devices with their start and end apart: 4, of which 2 were waited for; matrix products, arithmetic and copies ran while one was open for 0% of the time, Pallas kernels for 0%

commit v1 on v0

--- a/solution.py
+++ b/solution.py
@@ -104,7 +104,7 @@
     low_inverse, projected, lifted = jax.vmap(project_one)(sum_uu / cell_count, sum_ua / cell_count)
     residual = residual_rows(fields, basis_rows, lifted)
     local_rr = jnp.einsum("fsc,ftc->fst", residual, residual, precision=FULL_PRECISION)
-    sum_rr = lax.psum(local_rr, ("lon", "lat"))
+    sum_rr = jnp.sum(lax.all_gather(local_rr, ("lon", "lat")), axis=0)
     factor_up, up_inverse = jax.vmap(upper_pair)(sum_rr / cell_count)
     mix_old, mix_new, new_values = jax.vmap(rotate_one)(
         low_inverse, projected, factor_up, up_inverse, old_values

time: 1090 us -> 1050 us (0.963)
  blocking collectives: 116 us -> 77.4 us
    psum x1 -> x0, blocking collectives: 57.6 us -> none  [per_device(): sum_rr = lax.psum(local_rr, ('lon', 'lat'))]
    all_gather x0 -> x1, blocking collectives: none -> 18.7 us  [per_device(): sum_rr = jnp.sum(lax.all_gather(local_rr, ('lon', 'lat')), axis=0)]
where the time goes in v1:
time: 1050 us; the launch traced here: 1040 us
  other arithmetic  404 us (38%)
  local copies, waits for them, and re-layouts  308 us (29%)
  loops' own time  154 us (15%)
  matrix products  84 us (8%)
  blocking collectives  77.4 us (7%)
    while x448, local copies, waits for them, and re-layouts, row_step(): column = lax.dynamic_slice_in_dim(matrix, row, 1, 1)[:, 0]  286 us
    scatter x224, other arithmetic, row_step(): lax.dynamic_update_slice_in_dim(inverse, inverse_row[None], row, 0)  170 us
    another operation x224, other arithmetic  163 us
    another operation x4, loops' own time, cholesky_pair(): lax.fori_loop(0, order, row_step, (jnp.zeros_like(matrix), jnp.zeros_like...  154 us
    psum x1, blocking collectives, per_device(): sum_uu, sum_ua = lax.psum((local_uu, local_ua), ('lon', 'lat'))  58.7 us
    dot_general x224, matrix products, row_step(): partial_row = jnp.dot(inverse, column, precision=FULL_PRECISION)  43.8 us
    dot_general x224, matrix products, row_step(): jnp.dot(partial_row, inverse, precision=FULL_PRECISION)  35.1 us
    reduce_sum x224, other arithmetic, row_step(): pivot = jnp.sqrt(diag_entry - jnp.sum(partial_row * partial_row))  30 us
  transfers between devices with their start and end apart: 4, of which 2 were waited for; matrix products, arithmetic and copies ran while one was open for 0% of the time, Pallas kernels for 0%

profile of v1, /device:TPU:0, one launch (start us, length us, event | category | flops | bytes accessed | tf_op | source)
XLA Modules:
  0.0 1044.2 jit_solution(2059523237273608825)
XLA Ops:
  0.6 1.0 fusion.76
  1.7 6.0 collective-permute-start
  7.7 1.1 reshape.448
  10.0 4.3 collective-permute-done.1
  14.3 1.2 fusion.47
  15.7 1.3 collective-permute-start.2
  17.0 3.0 collective-permute-start.3
  20.1 0.9 collective-permute-done.3
  21.7 58.7 %all-reduce.1 = (f32[2,64,64]{2,1,0:T(8,128)S(1)}, f32[2,64,32]{1,2,0:T(8,128)S(1)}) all-reduce(f32[2,64,64]{2,1,0:T(8,128)S(1)} %fusion.78, f32[2,64,32]{1,2,0:T(8,128)S(1)} %convolution_bitcast_fusion), channel_id=1, replica_groups=mesh['level'=2,'lon'=8,'lat'=2] {'lon','lat'}, use_global_device_ids=true, to_apply=%region_0.0 | all-reduce | flops 12288 | bytes 98304 | tf_op jit(solution)/shard_map/psum | solution.py:103
  81.2 268.9 %while.71 = (s32[]{:T(128)}, f32[2,64,64]{2,0,1:T(2,128)S(1)}, f32[2,64,64]{0,2,1:T(8,128)S(1)}, s32[]{:T(128)}, s32[2]{0:T(128)S(1)}, /*index=5*/s32[1]{0:T(128)}, s32[3]{0:T(128)S(1)}, s32[]{:T(128)}, s32[]{:T(128)}) while((s32[]{:T(128)}, f32[2,64,64]{2,0,1:T(2,128)S(1)}, f32[2,64,64]{0,2,1:T(8,128)S(1)}, s32[]{:T(128)}, ...), condition=%wide.region_4.5_spmd.clone, body=%wide.region_1.4_spmd.clone.sunk | while | flops 197400 | bytes 75255 | solution.py:40
  351.3 18.7 %all-gather = f32[32,32,32]{2,1,0:T(8,128)S(1)} all-gather(f32[2,32,32]{2,1,0:T(8,128)S(1)} %fusion.80), channel_id=2, replica_groups=mesh['level'=2,'lon'=8,'lat'=2] {'lon','lat'}, dimensions={0}, use_global_device_ids=true | all-gather | bytes 139264 | tf_op jit(solution)/shard_map/all_gather | solution.py:107
  370.4 131.4 %while.72 = (s32[]{:T(128)}, f32[2,32,32]{2,0,1:T(2,128)S(1)}, f32[2,32,32]{2,0,1:T(2,128)S(1)}, f32[2,32,32]{0,2,1:T(8,128)S(1)}, s32[]{:T(128)}, /*index=5*/s3...) while((s32[]{:T(128)}, f32[2,32,32]{2,0,1:T(2,128)S(1)}, ...), condition=%wide.region_10.11_spmd.clone, body=%wide.region_7.10_spmd.clone.sunk | while | flops 49752 | bytes 26751 | solution.py:40
  373.7 0.8 constant_dynamic-update-slice_fusion.5
  377.8 0.8 constant_dynamic-update-slice_fusion.5
  382.0 0.8 constant_dynamic-update-slice_fusion.5
  386.1 0.8 constant_dynamic-update-slice_fusion.5
  390.2 0.8 constant_dynamic-update-slice_fusion.5
  394.3 0.8 constant_dynamic-update-slice_fusion.5
  398.4 0.8 constant_dynamic-update-slice_fusion.5
  410.7 0.8 constant_dynamic-update-slice_fusion.5
  414.8 0.8 constant_dynamic-update-slice_fusion.5
  418.9 0.8 constant_dynamic-update-slice_fusion.5
  423.0 0.8 constant_dynamic-update-slice_fusion.5
  427.1 0.8 constant_dynamic-update-slice_fusion.5
  431.2 0.8 constant_dynamic-update-slice_fusion.5
  435.3 0.8 constant_dynamic-update-slice_fusion.5
  439.4 0.8 constant_dynamic-update-slice_fusion.5
  451.8 0.8 constant_dynamic-update-slice_fusion.5
  455.9 0.8 constant_dynamic-update-slice_fusion.5
  503.5 267.9 %while.73 = (s32[]{:T(128)}, f32[2,64,64]{2,0,1:T(2,128)S(1)}, f32[2,64,64]{0,2,1:T(8,128)S(1)}, s32[]{:T(128)}, s32[2]{0:T(128)S(1)}, /*index=5*/s32[1]{0:T(128)}, s32[3]{0:T(128)S(1)}, s32[]{:T(128)}, s32[]{:T(128)}) while((s32[]{:T(128)}, f32[2,64,64]{2,0,1:T(2,128)S(1)}, f32[2,64,64]{0,2,1:T(8,128)S(1)}, s32[]{:T(128)}, ...), condition=%wide.region_14.15_spmd.clone, body=%wide.region_11.14_spmd.clone.sunk | while | flops 197400 | bytes 75255 | solution.py:40
  772.9 267.9 %while.74 = (s32[]{:T(128)}, f32[2,64,64]{2,0,1:T(2,128)S(1)}, f32[2,64,64]{0,2,1:T(8,128)S(1)}, s32[]{:T(128)}, s32[2]{0:T(128)S(1)}, /*index=5*/s32[1]{0:T(128)}, s32[3]{0:T(128)S(1)}, s32[]{:T(128)}, s32[]{:T(128)}) while((s32[]{:T(128)}, f32[2,64,64]{2,0,1:T(2,128)S(1)}, f32[2,64,64]{0,2,1:T(8,128)S(1)}, s32[]{:T(128)}, ...), condition=%wide.region_18.19_spmd.clone, body=%wide.region_15.0_spmd.clone.sunk | while | flops 197400 | bytes 75255 | solution.py:40
  1043.4 0.8 reshape.449
  (2727 shorter events, 778.7 us)
Async XLA Ops:
  1.7 8.3 collective-permute-start
  7.7 6.6 collective-permute-start.1
  15.7 4.4 collective-permute-start.2
  17.0 4.0 collective-permute-start.3
  20.1 61.1 %copy-start = (s32[2]{0:T(128)S(1)}, s32[2]{0:T(128)}, u32[]{:S(2)}) copy-start(s32[2]{0:T(128)} %constant.357.clone.2) | copy-start | bytes 28
  20.1 61.1 %copy-start.1 = (s32[3]{0:T(128)S(1)}, s32[3]{0:T(128)}, u32[]{:S(2)}) copy-start(s32[3]{0:T(128)} %constant.358.clone.2) | copy-start | bytes 40
  81.2 289.2 %copy-start.2 = (s32[2]{0:T(128)S(1)}, s32[2]{0:T(128)}, u32[]{:S(2)}) copy-start(s32[2]{0:T(128)} %constant.365.clone.2) | copy-start | bytes 28
  81.2 289.2 %copy-start.3 = (s32[3]{0:T(128)S(1)}, s32[3]{0:T(128)}, u32[]{:S(2)}) copy-start(s32[3]{0:T(128)} %constant.366.clone.2) | copy-start | bytes 40
